TPU v7x, 256 devices: a whole 4x4x8 slice. The times are simulated.
256 devices in a mesh: row: 2 (over core), blk: 128 (over y, z, x).
Axes of the slice: x: 4, y: 4, z: 8, core: 2. Of those that a mesh axis runs over, the one named last changes fastest.
Arguments:
- state: float32 [2, 5, 4096, 512], P('row', None, 'blk'), may hold values from -6 to 6
- forcing: float32 [2, 5, 4096, 512], P('row', None, 'blk'), may hold values from -6 to 6
- sigma: float32 [2, 4096, 512], P('row', 'blk'), may hold values from 0.05 to 2
- partner: int32 [2, 4096, 1], P('row', 'blk'), may hold values from 0 to 15; in each aligned block of 32 rows (0 to 31, 32 to 63, ..., all dimensions but the last counted through in order) at most 4 rows name the same one
- loop_weight: float32 [2, 1024], P('row'), may hold values from 0.05 to 0.2
- offset: int32 [1], replicated, may hold values from 0 to 1023
Outputs:
- solution: float32 [2, 5, 4096, 512], P('row', None, 'blk')
- loop_correction: float32 [2, 5, 1024], P('row', None, 'blk')
Inputs may be any that keep to these rules, and one draw needn't show every extreme that they name: Among the 32 face cells of one device no partner slot is named more than 4 times.
All inputs are finite; a program needn't handle non-finite values.
Results may differ from a plain program's by a relative error of at most 0.00011.
Values sent between devices are 32-bit elements; how exact they have to be, the bound alone decides.
A program may use at most 64 MiB of HBM per device.

v0:
```python
import jax
import jax.numpy as jnp
from jax import lax
from jax.sharding import PartitionSpec as P

SECTIONS1 = 3
SECTIONS2 = 3
SECTIONS3 = 4
COEFF = 0.8


def padded_2(cells, sides, width):
    for axis, dim in sides:
        count = lax.axis_size(axis)
        head = lax.slice_in_dim(cells, 0, width, axis=dim)
        tail = lax.slice_in_dim(cells, cells.shape[dim] - width, cells.shape[dim], axis=dim)
        cells = jnp.concatenate(
            [
                lax.ppermute(tail, axis, [(i, (i + 1) % count) for i in range(count)]),
                cells,
                lax.ppermute(head, axis, [((i + 1) % count, i) for i in range(count)]),
            ],
            axis=dim,
        )
    return cells


def from_partner(block, axis, distance):
    count = lax.axis_size(axis)
    route = []
    for low in range(count):
        high = low | 1 << distance
        if high != low and high < count:
            route += [(low, high), (high, low)]
    return lax.ppermute(block, axis, route)


def nonlinear(field):
    q = jnp.mean(field * field, axis=0, keepdims=True)
    return 0.5 * field * q / (1.0 + q)


def apply_operator(extended, sigma_in, scale):
    centre = extended[:, 1:-1]
    across = extended[:, 2:] + extended[:, :-2]
    padded = jnp.pad(centre, ((0, 0), (0, 0), (1, 1)))
    along = padded[:, :, 2:] + padded[:, :, :-2]
    return scale * (4.0 * centre - (across + along)) + sigma_in[None] * centre + nonlinear(centre)


def step_size(sigma_in, scale):
    return COEFF / (4.0 * scale + sigma_in + 1.5)


def smooth_section(field, source, sigma_in, scale, count, wanted):
    tau = step_size(sigma_in, scale)[None]
    start = field
    for section in range(count):
        extended = padded_2(field, (("blk", 1),), 1)
        field = start + 1.0 / (count - section) * tau * (
            source - apply_operator(extended, sigma_in, scale)
        )
    if wanted:
        extended = padded_2(field, (("blk", 1),), 1)
        return (field, source - apply_operator(extended, sigma_in, scale))
    return field


def smooth(field, source, sigma_in, scale, count, wanted):
    return smooth_section(field, source, sigma_in, scale, count, wanted)


def evaluate(field, sigma_in, scale):
    extended = padded_2(field, (("blk", 1),), 1)
    return apply_operator(extended, sigma_in, scale)


def coarsen(x):
    rows, cols = (x.shape[-2], x.shape[-1])
    return x.reshape(x.shape[:-2] + (rows // 2, 2, cols // 2, 2)).mean(axis=(-3, -1))


def refine(x):
    return jnp.repeat(jnp.repeat(x, 2, axis=-2), 2, axis=-1)


def body(state, forcing, sigma, partner, loop_weight, offset):
    row_index = lax.axis_index("row")
    f1 = forcing[0]
    s1 = sigma[0]
    u1, r1 = smooth(state[0], f1, s1, 1.0, SECTIONS1, True)
    face = jnp.where(row_index == 0, r1[:, :, -1], r1[:, :, 0])
    loop_cells = loop_weight.shape[1]
    block_count = lax.axis_size("blk")
    loop_cell = (partner[0, :, 0] * block_count + lax.axis_index("blk")) % loop_cells
    lookup = (loop_cell[:, None] == jnp.arange(loop_cells, dtype=jnp.int32)[None, :]).astype(
        jnp.float32
    )
    contrib = jnp.dot(face, lookup, precision=lax.Precision.HIGHEST)
    own_piece = lax.psum_scatter(contrib, "blk", scatter_dimension=1, tiled=True)
    other_piece = from_partner(own_piece, "row", 0)
    own_loop, other_loop = (
        lax.all_gather(own_piece, "blk", axis=1, tiled=True),
        lax.all_gather(other_piece, "blk", axis=1, tiled=True),
    )
    shift = jnp.where(row_index == 0, -offset[0], offset[0])
    rolled = jnp.roll(other_loop, shift, axis=1)
    correction = loop_weight[0][None, :] * (own_loop + rolled)
    face_fix = jnp.dot(correction, lookup.T, precision=lax.Precision.HIGHEST)
    s2 = coarsen(s1)
    s3 = coarsen(s2)
    u2_start = coarsen(u1)
    f2 = evaluate(u2_start, s2, 0.25) + coarsen(r1)
    u2, r2 = smooth(u2_start, f2, s2, 0.25, SECTIONS2, True)
    u3_start = coarsen(u2)
    f3 = evaluate(u3_start, s3, 0.0625) + coarsen(r2)
    u3 = smooth(u3_start, f3, s3, 0.0625, SECTIONS3, False)
    u2 = u2 + refine(u3 - u3_start)
    u2 = smooth(u2, f2, s2, 0.25, SECTIONS2, False)
    u1 = u1 + refine(u2 - u2_start)
    axial = u1.shape[2]
    columns = jnp.arange(axial, dtype=jnp.int32)
    target = jnp.where(row_index == 0, axial - 1, 0)
    column_mask = (columns == target).astype(jnp.float32)
    u1 = u1 + face_fix[:, :, None] * column_mask[None, None, :]
    u1 = smooth(u1, f1, s1, 1.0, SECTIONS1, False)
    segment = loop_cells // block_count
    loop_out = lax.dynamic_slice_in_dim(correction, lax.axis_index("blk") * segment, segment, 1)
    return (u1[None], loop_out[None])


def solution(mesh):
    placed = (
        P("row", None, "blk", None),
        P("row", None, "blk", None),
        P("row", "blk", None),
        P("row", "blk", None),
        P("row", None),
        P(),
    )
    return jax.shard_map(
        body,
        mesh=mesh,
        in_specs=placed,
        out_specs=(P("row", None, "blk", None), P("row", None, "blk")),
        check_vma=False,
    )
```

profile of v0, /device:TPU:0, one launch (start us, length us, event | category | flops | bytes accessed | tf_op | source)
XLA Modules:
  0.0 1750.3 jit_solution(17621509908090963667)
XLA Ops:
  5.7 8.8 collective-permute-start
  16.8 5.5 reshape_squeeze.3
  41.5 7.6 collective-permute-start.2
  53.9 6.5 multiply_reduce_fusion.4
  65.8 7.4 collective-permute-start.4
  77.7 6.4 multiply_reduce_fusion.3
  86.6 8.8 copy.463
  99.3 7.8 collective-permute-start.8
  107.1 10.8 reduce_sum.227
  132.4 688.9 %all-reduce.18 = f32[5,1024]{1,0:T(8,128)S(1)} all-reduce(f32[5,1024]{1,0:T(8,128)S(1)} %fusion.56), channel_id=2, replica_groups=mesh['row'=2,'blk'=128] {'blk'}, use_global_device_ids=true, to_apply=%region_21.22.clone | all-reduce | flops 5120 | bytes 40960
  821.5 8.8 copy.472
  830.2 10.8 reduce_sum.231
  846.8 366.0 %all_gather.6 = f32[5,1024]{0,1:T(8,128)} all-gather(f32[5,8]{0,1:T(8,128)S(1)} %copy.484), channel_id=1, replica_groups=mesh['row'=2,'blk'=128] {'blk'}, dimensions={1}, use_global_device_ids=true | all-gather | bytes 20640 | tf_op jit(solution)/shard_map/all_gather | solution.py:103
  1214.1 360.5 %all_gather.7 = f32[5,1024]{0,1:T(8,128)} all-gather(f32[5,8]{0,1:T(8,128)S(1)} %copy.485), channel_id=1, replica_groups=mesh['row'=2,'blk'=128] {'blk'}, dimensions={1}, use_global_device_ids=true | all-gather | bytes 20640 | tf_op jit(solution)/shard_map/all_gather | solution.py:104
  1581.3 7.6 collective-permute-done.13
  1613.2 6.1 collective-permute-start.18
  1620.6 7.7 collective-permute-done.19
  1632.1 5.5 collective-permute-done.21
  1641.4 5.7 collective-permute-done.23
  1684.4 7.4 collective-permute-start.31
  1705.2 7.8 collective-permute-start.33
  1717.4 5.8 multiply_reduce_fusion
  1728.6 7.8 collective-permute-start.35
  1740.8 6.7 fusion.8
  (253 shorter events, 174.6 us)
Async XLA Ops:
  5.2 25.3 %collective-permute-start.1 = (f32[5,1,512]{2,1,0:T(1,128)S(1)}, f32[5,1,512]{2,1,0:T(1,128)S(1)}, u32[]{:S(2)}, u32[]{:S(2)}) collective-permute-start(f32[5,1,512]{2,1,0:T(1,128)S(1)} %copy.452), channel_id=1, source_target_pairs={{0,1},{1,2},{2,3},{3,4},{4,5},{5,6},{6,7},{7,8},{8,9},{9,10},{10,1... | collective-permute-start | bytes 30728 | tf_op jit(solution)/shard_map/ppermute | solution.py:19
  5.7 23.3 %collective-permute-start = (f32[5,1,512]{2,1,0:T(1,128)S(1)}, f32[5,1,512]{2,1,0:T(1,128)S(1)}, u32[]{:S(2)}, u32[]{:S(2)}) collective-permute-start(f32[5,1,512]{2,1,0:T(1,128)S(1)} %copy.450), channel_id=1, source_target_pairs={{1,0},{2,1},{3,2},{4,3},{5,4},{6,5},{7,6},{8,7},{9,8},{10,9},{11,1... | collective-permute-start | bytes 30728 | tf_op jit(solution)/shard_map/ppermute | solution.py:21
  41.4 11.0 collective-permute-start.3
  41.5 9.4 collective-permute-start.2
  65.8 10.4 collective-permute-start.5
  99.2 27.2 %collective-permute-start.9 = (f32[5,1,512]{2,1,0:T(1,128)S(1)}, f32[5,1,512]{2,1,0:T(1,128)S(1)}, u32[]{:S(2)}, u32[]{:S(2)}) collective-permute-start(f32[5,1,512]{2,1,0:T(1,128)S(1)} %copy.470), channel_id=1, source_target_pairs={{0,1},{1,2},{2,3},{3,4},{4,5},{5,6},{6,7},{7,8},{8,9},{9,10},{10,1... | collective-permute-start | bytes 30728 | tf_op jit(solution)/shard_map/ppermute | solution.py:19
  99.3 25.7 %collective-permute-start.8 = (f32[5,1,512]{2,1,0:T(1,128)S(1)}, f32[5,1,512]{2,1,0:T(1,128)S(1)}, u32[]{:S(2)}, u32[]{:S(2)}) collective-permute-start(f32[5,1,512]{2,1,0:T(1,128)S(1)} %copy.468), channel_id=1, source_target_pairs={{1,0},{2,1},{3,2},{4,3},{5,4},{6,5},{7,6},{8,7},{9,8},{10,9},{11,1... | collective-permute-start | bytes 30728 | tf_op jit(solution)/shard_map/ppermute | solution.py:21
  120.7 722.6 %collective-permute-start.6 = (f32[5,1,256]{2,1,0:T(1,128)}, f32[5,1,256]{2,1,0:T(1,128)S(1)}, u32[]{:S(2)}, u32[]{:S(2)}) collective-permute-start(f32[5,1,256]{2,1,0:T(1,128)} %get-tuple-element.92), channel_id=1, source_target_pairs={{1,0},{2,1},{3,2},{4,3},{5,4},{6,5},{7,6},{8,7},{9,8},{10,9},{11,1... | collective-permute-start | bytes 15368 | tf_op jit(solution)/shard_map/ppermute | solution.py:21
  123.0 720.3 %collective-permute-start.7 = (f32[5,1,256]{2,1,0:T(1,128)}, f32[5,1,256]{2,1,0:T(1,128)S(1)}, u32[]{:S(2)}, u32[]{:S(2)}) collective-permute-start(f32[5,1,256]{2,1,0:T(1,128)} %get-tuple-element.93), channel_id=1, source_target_pairs={{0,1},{1,2},{2,3},{3,4},{4,5},{5,6},{6,7},{7,8},{8,9},{9,10},{10,1... | collective-permute-start | bytes 15368 | tf_op jit(solution)/shard_map/ppermute | solution.py:19
  821.5 392.6 %collective-permute-start.30 = (f32[5,8]{1,0:T(8,128)S(1)}, f32[5,8]{1,0:T(8,128)S(1)}, u32[]{:S(2)}, u32[]{:S(2)}) collective-permute-start(f32[5,8]{1,0:T(8,128)S(1)} %constant_dynamic-slice_fusion), channel_id=1, source_target_pairs={{0,128},{128,0},{1,129},{129,1},{2,130},{130,2},{3,131},{131,3},{4... | collective-permute-start | bytes 488 | tf_op jit(solution)/shard_map/ppermute | solution.py:35
  844.7 732.7 %collective-permute-start.10 = (f32[5,1,256]{2,1,0:T(1,128)S(1)}, f32[5,1,256]{2,1,0:T(1,128)S(1)}, u32[]{:S(2)}, u32[]{:S(2)}) collective-permute-start(f32[5,1,256]{2,1,0:T(1,128)S(1)} %get-tuple-element.88), channel_id=1, source_target_pairs={{1,0},{2,1},{3,2},{4,3},{5,4},{6,5},{7,6},{8,7},{9,8},{10,9},{11,1... | collective-permute-start | bytes 15368 | tf_op jit(solution)/shard_map/ppermute | solution.py:21
  844.8 732.6 %collective-permute-start.11 = (f32[5,1,256]{2,1,0:T(1,128)S(1)}, f32[5,1,256]{2,1,0:T(1,128)S(1)}, u32[]{:S(2)}, u32[]{:S(2)}) collective-permute-start(f32[5,1,256]{2,1,0:T(1,128)S(1)} %get-tuple-element.89), channel_id=1, source_target_pairs={{0,1},{1,2},{2,3},{3,4},{4,5},{5,6},{6,7},{7,8},{8,9},{9,10},{10,1... | collective-permute-start | bytes 15368 | tf_op jit(solution)/shard_map/ppermute | solution.py:19
  1579.7 9.2 collective-permute-start.13
  1591.0 13.0 collective-permute-start.16
  1591.0 13.0 collective-permute-start.17
  1598.5 13.1 collective-permute-start.14
  1637.8 9.3 collective-permute-start.23
  1649.9 9.1 collective-permute-start.25
  1659.3 9.1 collective-permute-start.27
  1684.3 10.4 collective-permute-start.32
  1704.9 11.0 collective-permute-start.34
  1705.2 9.2 collective-permute-start.33
  1728.5 10.8 collective-permute-start.36
  1728.6 9.2 collective-permute-start.35
  (46 other events, 3378.0 us)
where the time goes:
time: 1760 us; the launch traced here: 1750 us
  blocking collectives  1420 us (81%)
  local copies, waits for them, and re-layouts  107 us (6%)
  starting transfers between devices  86.5 us (5%)
  other arithmetic  80.1 us (5%)
  waiting for transfers between devices  57.1 us (3%)
    unnamed x1, blocking collectives  689 us
    all_gather x1, blocking collectives, body(): lax.all_gather(own_piece, 'blk', axis=1, tiled=True)  366 us
    all_gather x1, blocking collectives, body(): lax.all_gather(other_piece, 'blk', axis=1, tiled=True)  360 us
    ppermute x18, starting transfers between devices, padded_2(): lax.ppermute(head, axis, [((i + 1) % count, i) for i in range(count)])  71.2 us
    ppermute x18, waiting for transfers between devices, padded_2(): lax.ppermute(tail, axis, [(i, (i + 1) % count) for i in range(count)])  44.6 us
  transfers between devices with their start and end apart: 37, of which 19 were waited for; matrix products, arithmetic and copies ran while one was open for 5% of the time, Pallas kernels for 0%

commit v1 on v0

--- a/solution.py
+++ b/solution.py
@@ -100,7 +100,9 @@
     own_piece = lax.psum_scatter(contrib, "blk", scatter_dimension=1, tiled=True)
     other_piece = from_partner(own_piece, "row", 0)
     own_loop, other_loop = (
-        lax.all_gather(own_piece, "blk", axis=1, tiled=True),
+        jnp.concatenate(
+            lax.all_to_all(jnp.stack([own_piece] * lax.axis_size("blk")), "blk", 0, 0), axis=1
+        ),
         lax.all_gather(other_piece, "blk", axis=1, tiled=True),
     )
     shift = jnp.where(row_index == 0, -offset[0], offset[0])

time: 1760 us -> 1420 us (0.81)
  blocking collectives: 1420 us -> 1060 us
    all_gather x1 -> x0, blocking collectives: 366 us -> none  [body(): lax.all_gather(own_piece, 'blk', axis=1, tiled=True)]
  transfers between devices with their start and end apart: 37 -> 38, of which waited for: 19 -> 18; matrix products, arithmetic and copies ran while one was open for 5% -> 7% of each run, Pallas kernels for 0% -> 0%
where the time goes in v1:
time: 1420 us; the launch traced here: 1410 us
  blocking collectives  1060 us (75%)
  local copies, waits for them, and re-layouts  112 us (8%)
  starting transfers between devices  99 us (7%)
  other arithmetic  82 us (6%)
  waiting for transfers between devices  54.8 us (4%)
    unnamed x1, blocking collectives  689 us
    all_gather x1, blocking collectives, body(): lax.all_gather(other_piece, 'blk', axis=1, tiled=True)  368 us
    ppermute x18, starting transfers between devices, padded_2(): lax.ppermute(head, axis, [((i + 1) % count, i) for i in range(count)])  77.1 us
    ppermute x18, waiting for transfers between devices, padded_2(): lax.ppermute(tail, axis, [(i, (i + 1) % count) for i in range(count)])  42.3 us
    reduce_sum x6, other arithmetic, coarsen(): x.reshape(x.shape[:-2] + (rows // 2, 2, cols // 2, 2)).mean(axis=(-3, -1))  32.9 us
    reduce_sum x17, other arithmetic, nonlinear(): q = jnp.mean(field * field, axis=0, keepdims=True)  29 us
  transfers between devices with their start and end apart: 38, of which 18 were waited for; matrix products, arithmetic and copies ran while one was open for 7% of the time, Pallas kernels for 0%

profile of v1, /device:TPU:0, one launch (start us, length us, event | category | flops | bytes accessed | tf_op | source)
XLA Modules:
  0.0 1408.2 jit_solution(3042616793264835182)
XLA Ops:
  5.7 8.8 collective-permute-start
  16.8 5.6 reshape_squeeze.3
  41.6 7.6 collective-permute-start.2
  54.0 6.6 multiply_reduce_fusion.4
  66.1 7.4 collective-permute-start.4
  77.9 6.5 multiply_reduce_fusion.3
  87.0 8.7 copy.459
  99.6 7.8 collective-permute-start.8
  107.4 10.8 reduce_sum.227
  132.8 688.9 %all-reduce.18 = f32[5,1024]{1,0:T(8,128)S(1)} all-reduce(f32[5,1024]{1,0:T(8,128)S(1)} %fusion.56), channel_id=2, replica_groups=mesh['row'=2,'blk'=128] {'blk'}, use_global_device_ids=true, to_apply=%region_21.22.clone | all-reduce | flops 5120 | bytes 40960
  821.7 8.7 copy.468
  831.3 7.3 all-to-all-start
  838.6 10.8 reduce_sum.231
  853.1 7.3 collective-permute-start.10
  860.5 367.9 %all_gather.3 = f32[5,1024]{0,1:T(8,128)} all-gather(f32[5,8]{0,1:T(8,128)S(1)} %copy.481), channel_id=1, replica_groups=mesh['row'=2,'blk'=128] {'blk'}, dimensions={1}, use_global_device_ids=true | all-gather | bytes 20640 | tf_op jit(solution)/shard_map/all_gather | solution.py:106
  1234.3 5.5 collective-permute-done.13
  1264.1 6.1 collective-permute-start.18
  1271.5 7.7 collective-permute-done.19
  1283.0 5.5 collective-permute-done.21
  1341.4 7.7 collective-permute-start.31
  1362.8 7.8 collective-permute-start.33
  1375.0 5.9 multiply_reduce_fusion
  1386.3 7.8 collective-permute-start.35
  1398.5 6.8 fusion.8
  (257 shorter events, 183.6 us)
Async XLA Ops:
  5.2 25.4 %collective-permute-start.1 = (f32[5,1,512]{2,1,0:T(1,128)S(1)}, f32[5,1,512]{2,1,0:T(1,128)S(1)}, u32[]{:S(2)}, u32[]{:S(2)}) collective-permute-start(f32[5,1,512]{2,1,0:T(1,128)S(1)} %copy.448), channel_id=1, source_target_pairs={{0,1},{1,2},{2,3},{3,4},{4,5},{5,6},{6,7},{7,8},{8,9},{9,10},{10,1... | collective-permute-start | bytes 30728 | tf_op jit(solution)/shard_map/ppermute | solution.py:19
  5.7 23.4 %collective-permute-start = (f32[5,1,512]{2,1,0:T(1,128)S(1)}, f32[5,1,512]{2,1,0:T(1,128)S(1)}, u32[]{:S(2)}, u32[]{:S(2)}) collective-permute-start(f32[5,1,512]{2,1,0:T(1,128)S(1)} %copy.446), channel_id=1, source_target_pairs={{1,0},{2,1},{3,2},{4,3},{5,4},{6,5},{7,6},{8,7},{9,8},{10,9},{11,1... | collective-permute-start | bytes 30728 | tf_op jit(solution)/shard_map/ppermute | solution.py:21
  41.5 11.0 collective-permute-start.3
  41.6 9.4 collective-permute-start.2
  66.0 10.4 collective-permute-start.5
  99.5 27.3 %collective-permute-start.9 = (f32[5,1,512]{2,1,0:T(1,128)S(1)}, f32[5,1,512]{2,1,0:T(1,128)S(1)}, u32[]{:S(2)}, u32[]{:S(2)}) collective-permute-start(f32[5,1,512]{2,1,0:T(1,128)S(1)} %copy.466), channel_id=1, source_target_pairs={{0,1},{1,2},{2,3},{3,4},{4,5},{5,6},{6,7},{7,8},{8,9},{9,10},{10,1... | collective-permute-start | bytes 30728 | tf_op jit(solution)/shard_map/ppermute | solution.py:19
  99.6 25.7 %collective-permute-start.8 = (f32[5,1,512]{2,1,0:T(1,128)S(1)}, f32[5,1,512]{2,1,0:T(1,128)S(1)}, u32[]{:S(2)}, u32[]{:S(2)}) collective-permute-start(f32[5,1,512]{2,1,0:T(1,128)S(1)} %copy.464), channel_id=1, source_target_pairs={{1,0},{2,1},{3,2},{4,3},{5,4},{6,5},{7,6},{8,7},{9,8},{10,9},{11,1... | collective-permute-start | bytes 30728 | tf_op jit(solution)/shard_map/ppermute | solution.py:21
  121.0 730.6 %collective-permute-start.6 = (f32[5,1,256]{2,1,0:T(1,128)}, f32[5,1,256]{2,1,0:T(1,128)S(1)}, u32[]{:S(2)}, u32[]{:S(2)}) collective-permute-start(f32[5,1,256]{2,1,0:T(1,128)} %get-tuple-element.92), channel_id=1, source_target_pairs={{1,0},{2,1},{3,2},{4,3},{5,4},{6,5},{7,6},{8,7},{9,8},{10,9},{11,1... | collective-permute-start | bytes 15368 | tf_op jit(solution)/shard_map/ppermute | solution.py:21
  123.4 728.3 %collective-permute-start.7 = (f32[5,1,256]{2,1,0:T(1,128)}, f32[5,1,256]{2,1,0:T(1,128)S(1)}, u32[]{:S(2)}, u32[]{:S(2)}) collective-permute-start(f32[5,1,256]{2,1,0:T(1,128)} %get-tuple-element.93), channel_id=1, source_target_pairs={{0,1},{1,2},{2,3},{3,4},{4,5},{5,6},{6,7},{7,8},{8,9},{9,10},{10,1... | collective-permute-start | bytes 15368 | tf_op jit(solution)/shard_map/ppermute | solution.py:19
  830.5 29.9 %collective-permute-start.30 = (f32[5,8]{1,0:T(8,128)S(1)}, f32[5,8]{1,0:T(8,128)S(1)}, u32[]{:S(2)}, u32[]{:S(2)}) collective-permute-start(f32[5,8]{1,0:T(8,128)S(1)} %constant_dynamic-slice_fusion), channel_id=1, source_target_pairs={{0,128},{128,0},{1,129},{129,1},{2,130},{130,2},{3,131},{131,3},{4... | collective-permute-start | bytes 488 | tf_op jit(solution)/shard_map/ppermute | solution.py:35
  831.3 499.5 %all-to-all-start = ((f32[128,5,8]{2,1,0:T(8,128)}), f32[128,5,8]{2,1,0:T(8,128)}, u32[]{:S(2)}, u32[]{:S(2)}) async-start(f32[128,5,8]{2,1,0:T(8,128)} %stack.2), calls=%async_computation | async-start | bytes 1048576 | tf_op jit(solution)/shard_map/all_to_all | solution.py:104
  853.1 377.2 %collective-permute-start.10 = (f32[5,1,256]{2,1,0:T(1,128)S(1)}, f32[5,1,256]{2,1,0:T(1,128)S(1)}, u32[]{:S(2)}, u32[]{:S(2)}) collective-permute-start(f32[5,1,256]{2,1,0:T(1,128)S(1)} %get-tuple-element.88), channel_id=1, source_target_pairs={{1,0},{2,1},{3,2},{4,3},{5,4},{6,5},{7,6},{8,7},{9,8},{10,9},{11,1... | collective-permute-start | bytes 15368 | tf_op jit(solution)/shard_map/ppermute | solution.py:21
  860.4 369.8 %collective-permute-start.11 = (f32[5,1,256]{2,1,0:T(1,128)S(1)}, f32[5,1,256]{2,1,0:T(1,128)S(1)}, u32[]{:S(2)}, u32[]{:S(2)}) collective-permute-start(f32[5,1,256]{2,1,0:T(1,128)S(1)} %get-tuple-element.89), channel_id=1, source_target_pairs={{0,1},{1,2},{2,3},{3,4},{4,5},{5,6},{6,7},{7,8},{8,9},{9,10},{10,1... | collective-permute-start | bytes 15368 | tf_op jit(solution)/shard_map/ppermute | solution.py:19
  1230.7 9.1 collective-permute-start.13
  1241.9 13.0 collective-permute-start.16
  1241.9 13.0 collective-permute-start.17
  1249.4 13.1 collective-permute-start.14
  1300.8 9.1 collective-permute-start.25
  1310.2 9.1 collective-permute-start.27
  1341.4 10.6 collective-permute-start.32
  1362.8 10.8 collective-permute-start.34
  1362.8 9.2 collective-permute-start.33
  1386.3 10.8 collective-permute-start.36
  1386.3 9.2 collective-permute-start.35
  (48 other events, 1600.1 us)
